TPU v7x, 32 devices: a whole 2x2x4 slice. The times are simulated.
32 devices in a mesh: dp: 16 (over z, y, x), tensor: 2 (over core).
Axes of the slice: x: 2, y: 2, z: 4, core: 2. Of those that a mesh axis runs over, the one named last changes fastest.
Arguments:
- inputs: bfloat16 [32768, 768], P(('dp', 'tensor')), may hold values from -6 to 6
- out_grad: bfloat16 [32768, 768], P(('dp', 'tensor')), may hold values from -6 to 6
- lengths: int32 [16], P('dp'), may hold values from 1025 to 2048
- w_qkv: bfloat16 [3, 768, 768], P(None, 'dp', 'tensor'), may hold values from -0.21875 to 0.21875
- w_out: bfloat16 [768, 768], P('tensor', 'dp'), may hold values from -1.75 to 1.75
- w_up: bfloat16 [768, 3072], P('dp', 'tensor'), may hold values from -0.21875 to 0.21875
- w_down: bfloat16 [3072, 768], P('tensor', 'dp'), may hold values from -0.109375 to 0.109375
- gains: bfloat16 [2, 768], replicated, may hold values from 0.099609375 to 1.8984375
- shifts: bfloat16 [4, 768], replicated, may hold values from -3 to 3
- ff_bias: bfloat16 [3072], P('tensor'), may hold values from -3 to 3
Outputs:
- out: bfloat16 [32768, 768], P(('dp', 'tensor'))
- grad_inputs: float32 [32768, 768], P(('dp', 'tensor'))
- grad_qkv: float32 [3, 768, 768], P(None, 'dp', 'tensor')
- grad_out_proj: float32 [768, 768], P('tensor', 'dp')
- grad_up: float32 [768, 3072], P('dp', 'tensor')
- grad_down: float32 [3072, 768], P('tensor', 'dp')
- grad_gains: float32 [2, 768], replicated
- grad_shifts: float32 [4, 768], replicated
- grad_ff_bias: float32 [3072], P('tensor')
All inputs are finite; a program needn't handle non-finite values.
Results may differ from a plain program's by a relative error of at most 0.015.
The roundings to bfloat16 on the way count: a program that leaves them out, or rounds other values in their place, can miss the bound.
Values may be sent and summed in bfloat16 or wider, within the bound.
A program may use at most 192 MiB of HBM per device.

v0:
```python
import jax
import jax.numpy as jnp
from jax import lax
from jax.sharding import PartitionSpec as P

HD = 64
LEN = 2048
norm_eps = 1e-06
masked_score = -1e30


def layer_norm(hidden, gain, shift):
    center = hidden - jnp.mean(hidden, axis=-1, keepdims=True)
    spread = jnp.mean(center * center, axis=-1, keepdims=True)
    return center * lax.rsqrt(spread + norm_eps) * gain + shift


def exact_gelu(ff_pre):
    return jax.nn.gelu(ff_pre, approximate=False)


def softmax_rows(query_block, key_rows, key_mask):
    scores = jnp.einsum("qd,kd->qk", query_block, key_rows, preferred_element_type=jnp.float32)
    scores = jnp.where(key_mask[None, :], scores, masked_score)
    row_max = jnp.max(scores, axis=-1, keepdims=True)
    shifted = jnp.exp(scores - row_max)
    return shifted / jnp.sum(shifted, axis=-1, keepdims=True)


def heads_first(matrix, seq_count, head_count):
    return (
        matrix.reshape(seq_count, LEN, head_count, HD)
        .transpose(0, 2, 1, 3)
        .reshape(seq_count * head_count, LEN, HD)
    )


def heads_last(stacked, seq_count, head_count):
    return (
        stacked.reshape(seq_count, head_count, LEN, HD)
        .transpose(0, 2, 1, 3)
        .reshape(seq_count * LEN, head_count * HD)
    )


def attend_forward(member):
    query_rows, key_rows, value_rows, seq_len = member
    key_mask = jnp.arange(LEN, dtype=jnp.int32) < seq_len
    block_rows = min(512, LEN)

    def one_block(query_block):
        attn_probs = softmax_rows(query_block, key_rows, key_mask)
        return jnp.dot(
            attn_probs.astype(jnp.bfloat16), value_rows, preferred_element_type=jnp.float32
        )

    context = lax.map(one_block, query_rows.reshape(LEN // block_rows, block_rows, HD))
    return context.reshape(LEN, HD)


def attend_backward(member):
    query_rows, key_rows, value_rows, ctx_rows, seq_len = member
    key_mask = jnp.arange(LEN, dtype=jnp.int32) < seq_len
    block_rows = min(512, LEN)

    def one_step(totals, blocks):
        key_total, value_total = totals
        query_block, ctx_block = blocks
        attn_probs = softmax_rows(query_block, key_rows, key_mask)
        prob_grad = jnp.einsum(
            "qd,kd->qk", ctx_block, value_rows, preferred_element_type=jnp.float32
        )
        delta = jnp.sum(attn_probs * prob_grad, axis=-1, keepdims=True)
        score_grad = (attn_probs * (prob_grad - delta)).astype(jnp.bfloat16)
        query_part = jnp.einsum(
            "qk,kd->qd", score_grad, key_rows, preferred_element_type=jnp.float32
        )
        key_total = key_total + jnp.einsum(
            "qk,qd->kd", score_grad, query_block, preferred_element_type=jnp.float32
        )
        value_total = value_total + jnp.einsum(
            "qk,qd->kd",
            attn_probs.astype(jnp.bfloat16),
            ctx_block,
            preferred_element_type=jnp.float32,
        )
        return ((key_total, value_total), query_part)

    zeros_init = jnp.zeros((LEN, HD), jnp.float32)
    shaped = (LEN // block_rows, block_rows, HD)
    (key_grad, value_grad), query_grad = lax.scan(
        one_step, (zeros_init, zeros_init), (query_rows.reshape(shaped), ctx_rows.reshape(shaped))
    )
    return (query_grad.reshape(LEN, HD), key_grad, value_grad)


def body(inputs, out_grad, lengths, w_qkv, w_out, w_up, w_down, gains, shifts, ff_bias):
    score_scale = HD ** (-0.5)
    seq_count = lengths.shape[0]
    head_count = w_qkv.shape[2] // HD
    gains_f = gains.astype(jnp.float32)
    shifts_f = shifts.astype(jnp.float32)
    inputs_f = inputs.astype(jnp.float32)
    gathered = lax.all_gather(inputs, "tensor", axis=0, tiled=True)
    qkv_full, out_full = (
        lax.all_gather(w_qkv, "dp", axis=1, tiled=True),
        lax.all_gather(w_out, "dp", axis=1, tiled=True),
    )
    projected = jnp.einsum("rd,cde->cre", gathered, qkv_full, preferred_element_type=jnp.float32)
    queries = (projected[0] * score_scale).astype(jnp.bfloat16)
    keys_all = projected[1].astype(jnp.bfloat16)
    values_all = projected[2].astype(jnp.bfloat16)
    head_lens = jnp.repeat(lengths, head_count)
    query_heads = heads_first(queries, seq_count, head_count)
    key_heads = heads_first(keys_all, seq_count, head_count)
    value_heads = heads_first(values_all, seq_count, head_count)
    context_f = lax.map(attend_forward, (query_heads, key_heads, value_heads, head_lens))
    context = heads_last(context_f, seq_count, head_count).astype(jnp.bfloat16)
    attn_branch = (
        lax.psum_scatter(
            jnp.dot(context, out_full, preferred_element_type=jnp.float32),
            "tensor",
            scatter_dimension=0,
            tiled=True,
        )
        + shifts_f[0]
    )
    resid_one = inputs_f + attn_branch
    normed_f, norm_one_back = jax.vjp(layer_norm, resid_one, gains_f[0], shifts_f[1])
    normed_one = normed_f.astype(jnp.bfloat16)
    normed_all = lax.all_gather(normed_one, "tensor", axis=0, tiled=True)
    up_full, down_full = (
        lax.all_gather(w_up, "dp", axis=0, tiled=True),
        lax.all_gather(w_down, "dp", axis=1, tiled=True),
    )
    ff_pre = jnp.dot(normed_all, up_full, preferred_element_type=jnp.float32) + ff_bias.astype(
        jnp.float32
    )
    ff_act_f, gelu_back = jax.vjp(exact_gelu, ff_pre)
    ff_act = ff_act_f.astype(jnp.bfloat16)
    mlp_branch = (
        lax.psum_scatter(
            jnp.dot(ff_act, down_full, preferred_element_type=jnp.float32),
            "tensor",
            scatter_dimension=0,
            tiled=True,
        )
        + shifts_f[2]
    )
    resid_two = normed_one.astype(jnp.float32) + mlp_branch
    result, norm_two_back = jax.vjp(layer_norm, resid_two, gains_f[1], shifts_f[3])
    resid_two_grad, gain_two_grad, shift_three_grad = norm_two_back(out_grad.astype(jnp.float32))
    mlp_grad = resid_two_grad.astype(jnp.bfloat16)
    shift_two_grad = jnp.sum(mlp_grad.astype(jnp.float32), axis=0)
    mlp_grad_all = lax.all_gather(mlp_grad, "tensor", axis=0, tiled=True)
    act_grad = jnp.einsum("rd,fd->rf", mlp_grad_all, down_full, preferred_element_type=jnp.float32)
    down_grad = jnp.einsum("rf,rd->fd", ff_act, mlp_grad_all, preferred_element_type=jnp.float32)
    pre_grad = gelu_back(act_grad)[0].astype(jnp.bfloat16)
    bias_grad = jnp.sum(pre_grad.astype(jnp.float32), axis=0)
    up_grad = jnp.einsum("rd,rf->df", normed_all, pre_grad, preferred_element_type=jnp.float32)
    slab_rows = pre_grad
    normed_grad = resid_two_grad + lax.psum_scatter(
        jnp.einsum("rf,df->rd", slab_rows, up_full, preferred_element_type=jnp.float32),
        "tensor",
        scatter_dimension=0,
        tiled=True,
    )
    resid_one_grad, gain_one_grad, shift_one_grad = norm_one_back(normed_grad)
    attn_grad = resid_one_grad.astype(jnp.bfloat16)
    shift_zero_grad = jnp.sum(attn_grad.astype(jnp.float32), axis=0)
    attn_grad_all = lax.all_gather(attn_grad, "tensor", axis=0, tiled=True)
    context_grad = jnp.einsum(
        "rd,ed->re", attn_grad_all, out_full, preferred_element_type=jnp.float32
    ).astype(jnp.bfloat16)
    out_proj_grad = jnp.einsum(
        "re,rd->ed", context, attn_grad_all, preferred_element_type=jnp.float32
    )
    ctx_heads = heads_first(context_grad, seq_count, head_count)
    query_grad, key_grad, value_grad = lax.map(
        attend_backward, (query_heads, key_heads, value_heads, ctx_heads, head_lens)
    )
    stacked_grad = jnp.stack(
        [
            heads_last(query_grad, seq_count, head_count),
            heads_last(key_grad, seq_count, head_count),
            heads_last(value_grad, seq_count, head_count),
        ]
    ).astype(jnp.bfloat16)
    qkv_scale = jnp.array([score_scale, 1.0, 1.0], jnp.float32)
    qkv_grad = (
        jnp.einsum("rd,cre->cde", gathered, stacked_grad, preferred_element_type=jnp.float32)
        * qkv_scale[:, None, None]
    )
    qkv_owned, out_owned, up_owned, down_owned = (
        lax.psum_scatter(qkv_grad, "dp", scatter_dimension=1, tiled=True),
        lax.psum_scatter(out_proj_grad, "dp", scatter_dimension=1, tiled=True),
        lax.psum_scatter(up_grad, "dp", scatter_dimension=0, tiled=True),
        lax.psum_scatter(down_grad, "dp", scatter_dimension=1, tiled=True),
    )
    slab_rows = stacked_grad
    parts = jnp.einsum("cre,cde->crd", slab_rows, qkv_full, preferred_element_type=jnp.float32)
    input_grad = resid_one_grad + lax.psum_scatter(
        (parts[0] * score_scale + parts[1] + parts[2]).astype(jnp.bfloat16),
        "tensor",
        scatter_dimension=0,
        tiled=True,
    ).astype(jnp.float32)
    gain_grads = jnp.stack([gain_one_grad, gain_two_grad])
    shift_grads = jnp.stack([shift_zero_grad, shift_one_grad, shift_two_grad, shift_three_grad])
    tensor_count = lax.axis_size("tensor")
    own_slot = (jnp.arange(tensor_count, dtype=jnp.int32) == lax.axis_index("tensor")).astype(
        jnp.float32
    )
    spread_bias = own_slot[:, None] * bias_grad[None, :]
    gain_sum, shift_sum, bias_sum = lax.psum(
        (gain_grads, shift_grads, spread_bias), ("dp", "tensor")
    )
    bias_owned = jnp.sum(own_slot[:, None] * bias_sum, axis=0)
    return (
        result.astype(jnp.bfloat16),
        input_grad,
        qkv_owned,
        out_owned,
        up_owned,
        down_owned,
        gain_sum,
        shift_sum,
        bias_owned,
    )


def solution(mesh):
    return jax.shard_map(
        body,
        mesh=mesh,
        in_specs=(
            P(("dp", "tensor"), None),
            P(("dp", "tensor"), None),
            P("dp"),
            P(None, "dp", "tensor"),
            P("tensor", "dp"),
            P("dp", "tensor"),
            P("tensor", "dp"),
            P(),
            P(),
            P("tensor"),
        ),
        out_specs=(
            P(("dp", "tensor"), None),
            P(("dp", "tensor"), None),
            P(None, "dp", "tensor"),
            P("tensor", "dp"),
            P("dp", "tensor"),
            P("tensor", "dp"),
            P(),
            P(),
            P("tensor"),
        ),
        check_vma=False,
    )
```

profile of v0, /device:TPU:0, one launch (start us, length us, event | category | flops | bytes accessed | tf_op | source)
XLA Modules:
  0.0 1468.2 jit_solution(2063813809935758152)
XLA Ops:
  9.4 48.6 %all_gather.26 = bf16[384,768]{0,1:T(8,128)(2,1)} all-gather(bf16[384,48]{0,1:T(8,128)(2,1)} %param.23), channel_id=1, replica_groups=mesh['dp'=16,'tensor'=2] {'dp'}, dimensions={1}, use_global_device_ids=true | all-gather | bytes 626688 | tf_op jit(solution)/shard_map/all_gather | solution.py:107
  58.0 29.4 %all-gather.8.cloned.1.call-done = bf16[3,768,384]{2,1,0:T(8,128)(2,1)} async-done(((bf16[3,48,384]{2,1,0:T(8,128)(2,1)}), bf16[3,768,384]{2,1,0:T(8,128)(2,1)}) %all-gather.8.cloned.1.call-update) | async-done | bytes 1769488 | tf_op jit(solution)/shard_map/all_gather | solution.py:106
  87.4 9.9 fusion.61
  108.1 103.9 %while.51 = (s32[]{:T(128)}, bf16[6,2048,64]{1,2,0:T(8,128)(2,1)S(1)}, bf16[6,2048,64]{2,1,0:T(8,128)(2,1)}, bf16[6,2048,64]{2,1,0:T(8,128)(2,1)}, s32[6]{0:T(12...) while((s32[]{:T(128)}, bf16[6,2048,64]{1,2,0:T(8,128)(2,1)S(1)}, ...), condition=%wide.region_5.6_spmd, body=%wide.region_0.5_spmd.sunk | while | flops 277873664 | bytes 17058060 | solution.py:117
  111.1 13.8 while.54
  128.4 13.8 while.54
  145.7 13.8 while.54
  163.1 13.8 while.54
  180.4 13.8 while.54
  197.7 13.8 while.54
  212.1 6.0 fusion.62
  219.1 12.5 reduce-scatter.8.cloned.1.call-done
  237.9 60.2 %all-gather.14.cloned.1.call-done = bf16[768,1536]{1,0:T(8,128)(2,1)} async-done(((bf16[48,1536]{1,0:T(8,128)(2,1)}), bf16[768,1536]{1,0:T(8,128)(2,1)}) %all-gather.14.cloned.1.call-update) | async-done | bytes 2359312 | tf_op jit(solution)/shard_map/all_gather | solution.py:133
  298.1 13.0 all-gather.12.cloned.1.call-done
  311.1 34.9 %multiply_convert_fusion.1 = (bf16[2048,1536]{1,0:T(8,128)(2,1)}, f32[2048,1536]{1,0:T(8,128)}, f32[2048,1536]{1,0:T(8,128)}) fusion(f32[1536]{0:T(1024)S(1)} %convert_element_type.134, bf16[2048,768]{1,0:T(8,128)(2,1)} %all-gather.12.cloned.1.call-done, bf16[768,1536]{1,0:T(8,128)(2,1)} %all-gather.14.cloned.1.call-done), kind=kOutput, calls=%fused_computation.56 | convolution fusion | flops 5039456256 | bytes 36968448 | tf_op jit(solution)/shard_map/dot_general | solution.py:136
  346.0 31.7 %all-gather.16.cloned.1.call-done = bf16[1536,768]{0,1:T(8,128)(2,1)} async-done(((bf16[1536,48]{0,1:T(8,128)(2,1)}), bf16[1536,768]{0,1:T(8,128)(2,1)}) %all-gather.16.cloned.1.call-update) | async-done | bytes 2359312 | tf_op jit(solution)/shard_map/all_gather | solution.py:134
  377.6 9.6 fusion.63
  387.6 13.2 reduce-scatter.10.cloned.1.call-done
  413.3 13.4 all-gather.18.cloned.1.call-done
  426.6 17.6 %convert_reduce_fusion = (f32[1536]{0:T(1024)}, bf16[2048,1536]{1,0:T(8,128)(2,1)S(1)}) fusion(f32[2048,1536]{1,0:T(8,128)} %get-tuple-element.382, bf16[2048,768]{1,0:T(8,128)(2,1)} %all-gather.18.cloned.1.call-done, bf16[1536,768]{0,1:T(8,128)(2,1)} %all-gather.16.cloned.1.call-done, f32[2048,1536]{1,0:T(8,128)} %get-tuple-element.400, ...), kind=kOutput, calls=%fused_computation.54 | convolution fusion | flops 4885314048 | bytes 36974592 | tf_op jit(solution)/shard_map/rd,fd->rf/dot_general | solution.py:156
  446.9 6.9 fusion.64
  453.9 15.8 %reduce-scatter.12.cloned.1.call-done = f32[1024,768]{1,0:T(8,128)} async-done(((f32[2048,768]{1,0:T(8,128)}), f32[1024,768]{1,0:T(8,128)}) %reduce-scatter.12.cloned.1.call-update) | async-done | bytes 3145744 | tf_op jit(solution)/shard_map/reduce_scatter | solution.py:162
  469.6 4.3 multiply_reduce_fusion.1
  479.2 13.4 all-gather.20.cloned.1.call-done
  503.3 328.2 %while.53 = (s32[]{:T(128)}, bf16[6,2048,64]{1,2,0:T(8,128)(2,1)}, bf16[6,2048,64]{1,2,0:T(8,128)(2,1)}, bf16[6,2048,64]{1,2,0:T(8,128)(2,1)}, bf16[6,2048,64]{2...) while((s32[]{:T(128)}, bf16[6,2048,64]{1,2,0:T(8,128)(2,1)}, ...), condition=%wide.region_23.24_spmd, body=%wide.region_17.23_spmd.sunk | while | flops 692584960 | bytes 79334840 | solution.py:179
  508.2 47.7 %while.55 = (s32[]{:T(128)}, f32[2048,64]{0,1:T(8,128)S(1)}, f32[2048,64]{0,1:T(8,128)S(1)}, bf16[4,512,64]{1,2,0:T(8,128)(2,1)S(1)}, bf16[4,512,64]{2,1,0:T(8,1...) while((s32[]{:T(128)}, f32[2048,64]{0,1:T(8,128)S(1)}, ...), condition=%wide.region_22.22_spmd.clone, body=%wide.region_18.21_spmd.clone.sunk | while | flops 692584960 | bytes 73566400 | solution.py:91
  524.4 3.5 convolution_add_fusion.5
  536.4 3.5 convolution_add_fusion.5
  548.3 3.5 convolution_add_fusion.5
  562.9 47.7 %while.55 = (s32[]{:T(128)}, f32[2048,64]{0,1:T(8,128)S(1)}, f32[2048,64]{0,1:T(8,128)S(1)}, bf16[4,512,64]{1,2,0:T(8,128)(2,1)S(1)}, bf16[4,512,64]{2,1,0:T(8,1...) while((s32[]{:T(128)}, f32[2048,64]{0,1:T(8,128)S(1)}, ...), condition=%wide.region_22.22_spmd.clone, body=%wide.region_18.21_spmd.clone.sunk | while | flops 692584960 | bytes 73566400 | solution.py:91
  579.1 3.5 convolution_add_fusion.5
  591.1 3.5 convolution_add_fusion.5
  603.0 3.5 convolution_add_fusion.5
  617.6 47.7 %while.55 = (s32[]{:T(128)}, f32[2048,64]{0,1:T(8,128)S(1)}, f32[2048,64]{0,1:T(8,128)S(1)}, bf16[4,512,64]{1,2,0:T(8,128)(2,1)S(1)}, bf16[4,512,64]{2,1,0:T(8,1...) while((s32[]{:T(128)}, f32[2048,64]{0,1:T(8,128)S(1)}, ...), condition=%wide.region_22.22_spmd.clone, body=%wide.region_18.21_spmd.clone.sunk | while | flops 692584960 | bytes 73566400 | solution.py:91
  622.0 3.5 convolution_add_fusion.5
  633.9 3.5 convolution_add_fusion.5
  645.8 3.5 convolution_add_fusion.5
  657.7 3.5 convolution_add_fusion.5
  672.4 47.7 %while.55 = (s32[]{:T(128)}, f32[2048,64]{0,1:T(8,128)S(1)}, f32[2048,64]{0,1:T(8,128)S(1)}, bf16[4,512,64]{1,2,0:T(8,128)(2,1)S(1)}, bf16[4,512,64]{2,1,0:T(8,1...) while((s32[]{:T(128)}, f32[2048,64]{0,1:T(8,128)S(1)}, ...), condition=%wide.region_22.22_spmd.clone, body=%wide.region_18.21_spmd.clone.sunk | while | flops 692584960 | bytes 73566400 | solution.py:91
  676.7 3.5 convolution_add_fusion.5
  688.6 3.5 convolution_add_fusion.5
  700.5 3.5 convolution_add_fusion.5
  712.4 3.5 convolution_add_fusion.5
  727.0 47.7 %while.55 = (s32[]{:T(128)}, f32[2048,64]{0,1:T(8,128)S(1)}, f32[2048,64]{0,1:T(8,128)S(1)}, bf16[4,512,64]{1,2,0:T(8,128)(2,1)S(1)}, bf16[4,512,64]{2,1,0:T(8,1...) while((s32[]{:T(128)}, f32[2048,64]{0,1:T(8,128)S(1)}, ...), condition=%wide.region_22.22_spmd.clone, body=%wide.region_18.21_spmd.clone.sunk | while | flops 692584960 | bytes 73566400 | solution.py:91
  743.3 3.5 convolution_add_fusion.5
  755.2 3.5 convolution_add_fusion.5
  767.1 3.5 convolution_add_fusion.5
  781.7 47.7 %while.55 = (s32[]{:T(128)}, f32[2048,64]{0,1:T(8,128)S(1)}, f32[2048,64]{0,1:T(8,128)S(1)}, bf16[4,512,64]{1,2,0:T(8,128)(2,1)S(1)}, bf16[4,512,64]{2,1,0:T(8,1...) while((s32[]{:T(128)}, f32[2048,64]{0,1:T(8,128)S(1)}, ...), condition=%wide.region_22.22_spmd.clone, body=%wide.region_18.21_spmd.clone.sunk | while | flops 692584960 | bytes 73566400 | solution.py:91
  786.1 3.5 convolution_add_fusion.5
  798.0 3.5 convolution_add_fusion.5
  809.9 3.5 convolution_add_fusion.5
  821.8 3.5 convolution_add_fusion.5
  837.9 8.2 multiply_bitcast_fusion
  846.0 6.3 copy.78
  852.6 7.1 fusion.50
  864.0 9.5 fusion.67
  875.4 9.6 fusion.66
  885.2 5.5 fusion.65
  892.1 42.1 %all-reduce.1 = (f32[2,768]{1,0:T(2,128)}, f32[4,768]{1,0:T(4,128)}, f32[2,1536]{1,0:T(2,128)S(1)}) all-reduce(f32[2,768]{1,0:T(2,128)S(1)} %pad_maximum_fusion.4, f32[4,768]{1,0:T(4,128)S(1)} %pad_maximum_fusion.3, f32[2,1536]{1,0:T(2,128)S(1)} %broadcast_multiply_fusion), channel_id=1, replica_groups=mesh['dp'=16,'tensor'=2] {'dp','tensor'}, use_global_device_ids=true, to_apply=%region_31.32 | all-reduce | flops 7680 | bytes 61440 | tf_op jit(solution)/shard_map/psum | solution.py:215
  934.9 98.8 %all-reduce.4.cloned.1.call-done = f32[3,768,384]{2,0,1:T(4,128)} async-done(((f32[3,768,384]{2,0,1:T(4,128)}), f32[3,768,384]{2,0,1:T(4,128)}) %all-reduce.4.cloned.1.call-update) | async-done | bytes 3538960
  1035.4 10.9 reduce-scatter.14.cloned.1.call-done
  1049.8 141.5 %reduce-scatter.20.cloned.1.call-done = f32[1536,48]{0,1:T(8,128)} async-done(((f32[1536,768]{0,1:T(8,128)}), f32[1536,48]{0,1:T(8,128)}) %reduce-scatter.20.cloned.1.call-update) | async-done | bytes 294928 | tf_op jit(solution)/shard_map/reduce_scatter | solution.py:198
  1191.3 141.8 %reduce-scatter.18.cloned.1.call-done = f32[48,1536]{1,0:T(8,128)} async-done(((f32[768,1536]{1,0:T(8,128)}), f32[48,1536]{1,0:T(8,128)}) %reduce-scatter.18.cloned.1.call-update) | async-done | bytes 294928 | tf_op jit(solution)/shard_map/reduce_scatter | solution.py:197
  1333.0 128.4 %reduce-scatter.16.cloned.1.call-done = f32[384,48]{0,1:T(8,128)} async-done(((f32[384,768]{0,1:T(8,128)}), f32[384,48]{0,1:T(8,128)}) %reduce-scatter.16.cloned.1.call-update) | async-done | bytes 73744 | tf_op jit(solution)/shard_map/reduce_scatter | solution.py:196
  (618 shorter events, 427.0 us)
Async XLA Ops:
  7.2 50.8 %all-gather.10.cloned.1.call-start = ((), (), s32[]{:S(2)}) async-start(), calls=%async_computation.8 | async-start | bytes 4718592 | tf_op jit(solution)/shard_map/all_gather | solution.py:104
  7.9 79.5 %all-gather.8.cloned.1.call-start = ((), (), s32[]{:S(2)}) async-start(), calls=%async_computation.7 | async-start | bytes 1880064 | tf_op jit(solution)/shard_map/all_gather | solution.py:106
  8.7 222.9 %reduce-scatter.8.cloned.1.call-start = ((), (), s32[]{:S(2)}) async-start(), calls=%async_computation.9 | async-start | bytes 9437184 | tf_op jit(solution)/shard_map/reduce_scatter | solution.py:120
  212.1 6.0 copy-start.5
  212.1 6.0 copy-start.26
  218.1 80.0 %all-gather.14.cloned.1.call-start = ((), (), s32[]{:S(2)}) async-start(), calls=%async_computation.11 | async-start | bytes 2506752 | tf_op jit(solution)/shard_map/all_gather | solution.py:133
  218.7 92.4 %all-gather.12.cloned.1.call-start = ((), (), s32[]{:S(2)}) async-start(), calls=%async_computation.10 | async-start | bytes 4718592 | tf_op jit(solution)/shard_map/all_gather | solution.py:131
  235.5 2.4 copy-start.20
  237.2 140.4 %all-gather.16.cloned.1.call-start = ((), (), s32[]{:S(2)}) async-start(), calls=%async_computation.12 | async-start | bytes 2506752 | tf_op jit(solution)/shard_map/all_gather | solution.py:134
  237.8 163.0 %reduce-scatter.10.cloned.1.call-start = ((), (), s32[]{:S(2)}) async-start(), calls=%async_computation.13 | async-start | bytes 9437184 | tf_op jit(solution)/shard_map/reduce_scatter | solution.py:142
  387.3 39.3 %all-gather.18.cloned.1.call-start = ((), (), s32[]{:S(2)}) async-start(), calls=%async_computation.14 | async-start | bytes 4718592 | tf_op jit(solution)/shard_map/all_gather | solution.py:155
  413.2 56.4 %reduce-scatter.12.cloned.1.call-start = ((), (), s32[]{:S(2)}) async-start(), calls=%async_computation.15 | async-start | bytes 9437184 | tf_op jit(solution)/shard_map/reduce_scatter | solution.py:162
  426.6 20.2 %copy-start.24 = (bf16[768,1536]{1,0:T(8,128)(2,1)S(1)}, bf16[768,1536]{1,0:T(8,128)(2,1)}, u32[]{:S(2)}) copy-start(bf16[768,1536]{1,0:T(8,128)(2,1)} %all-gather.14.cloned.1.call-done) | copy-start | bytes 7077892
  444.2 2.7 copy-start.29
  453.8 20.1 %copy-start.11 = (f32[1024]{0:T(1024)S(1)}, f32[1024]{0:T(1024)}, u32[]{:S(2)}) copy-start(f32[1024]{0:T(1024)} %copy-done.10) | copy-start | bytes 12292
  453.8 38.8 %all-gather.20.cloned.1.call-start = ((), (), s32[]{:S(2)}) async-start(), calls=%async_computation.16 | async-start | bytes 4718592 | tf_op jit(solution)/shard_map/all_gather | solution.py:171
  475.4 3.7 copy-start.8
  477.0 15.6 %copy-start.7 = (bf16[384,768]{0,1:T(8,128)(2,1)S(1)}, bf16[384,768]{0,1:T(8,128)(2,1)}, u32[]{:S(2)}) copy-start(bf16[384,768]{0,1:T(8,128)(2,1)} %all_gather.26) | copy-start | bytes 1769476
  479.2 554.5 %all-reduce.4.cloned.1.call-start = ((), (), s32[]{:S(2)}) async-start(), calls=%async_computation.21 | async-start | bytes 9437184
  499.2 4.0 copy-start.27
  509.7 2.0 copy-start
  512.5 3.5 copy-start.1
  521.6 2.0 copy-start
  524.4 3.5 copy-start.1
  533.5 2.0 copy-start
  536.4 3.5 copy-start.1
  545.4 2.0 copy-start
  548.3 3.5 copy-start.1
  564.4 2.0 copy-start
  567.2 3.5 copy-start.1
  579.1 3.5 copy-start.1
  591.1 3.5 copy-start.1
  603.0 3.5 copy-start.1
  622.0 3.5 copy-start.1
  633.9 3.5 copy-start.1
  645.8 3.5 copy-start.1
  657.7 3.5 copy-start.1
  676.7 3.5 copy-start.1
  688.6 3.5 copy-start.1
  700.5 3.5 copy-start.1
  712.4 3.5 copy-start.1
  731.3 3.5 copy-start.1
  743.3 3.5 copy-start.1
  755.2 3.5 copy-start.1
  767.1 3.5 copy-start.1
  786.0 3.5 copy-start.1
  798.0 3.5 copy-start.1
  809.9 3.5 copy-start.1
  821.8 3.5 copy-start.1
  833.4 4.5 copy-start.28
  852.4 194.0 %reduce-scatter.14.cloned.1.call-start = ((), (), s32[]{:S(2)}) async-start(), calls=%async_computation.17 | async-start | bytes 4718592 | tf_op jit(solution)/shard_map/reduce_scatter | solution.py:202
  862.1 329.1 %reduce-scatter.20.cloned.1.call-start = ((), (), s32[]{:S(2)}) async-start(), calls=%async_computation.20 | async-start | bytes 5013504 | tf_op jit(solution)/shard_map/reduce_scatter | solution.py:198
  873.5 459.5 %reduce-scatter.18.cloned.1.call-start = ((), (), s32[]{:S(2)}) async-start(), calls=%async_computation.19 | async-start | bytes 5013504 | tf_op jit(solution)/shard_map/reduce_scatter | solution.py:197
  885.0 5.7 copy-start.25
  885.0 6.9 copy-start.16
  885.0 6.9 copy-start.15
  885.1 6.9 copy-start.14
  885.1 6.9 copy-start.18
  885.1 7.0 copy-start.17
  885.1 7.0 copy-start.13
  885.1 7.0 copy-start.12
  885.1 161.3 %copy-start.9 = (f32[1024]{0:T(1024)S(1)}, f32[1024]{0:T(1024)}, u32[]{:S(2)}) copy-start(f32[1024]{0:T(1024)} %copy-done.8) | copy-start | bytes 12292
  885.1 576.3 %reduce-scatter.16.cloned.1.call-start = ((), (), s32[]{:S(2)}) async-start(), calls=%async_computation.18 | async-start | bytes 1253376 | tf_op jit(solution)/shard_map/reduce_scatter | solution.py:196
  885.2 161.2 %copy-start.3 = (f32[1024,768]{1,0:T(8,128)S(1)}, f32[1024,768]{1,0:T(8,128)}, u32[]{:S(2)}) copy-start(f32[1024,768]{1,0:T(8,128)} %copy-done.2) | copy-start | bytes 9437188
  (27 other events, 49.5 us)
Sparse Core Ops, SparseCore 0:
  9.6 14.8 all-gather.9
  27.1 60.2 all-gather.7
  218.3 13.2 reduce-scatter.7
  234.6 63.4 all-gather.13
  300.1 10.9 all-gather.11
  314.1 63.4 all-gather.15
  387.4 13.3 reduce-scatter.9
  413.3 13.2 all-gather.17
  453.9 15.6 reduce-scatter.11
  479.3 13.2 all-gather.19
  852.5 181.1 all-reduce.3
  1036.4 9.9 reduce-scatter.13
  1052.9 138.3 reduce-scatter.19
  1196.9 136.1 reduce-scatter.17
  1338.9 122.4 reduce-scatter.15
where the time goes:
time: 1480 us; the launch traced here: 1470 us
  waiting for transfers between devices  727 us (49%)
  matrix products  341 us (23%)
  local copies, waits for them, and re-layouts  154 us (10%)
  other arithmetic  136 us (9%)
  blocking collectives  90.7 us (6%)
  between operations  15.8 us (1%)
    reduce_scatter x1, waiting for transfers between devices, body(): lax.psum_scatter(up_grad, 'dp', scatter_dimension=0, tiled=True)  142 us
    reduce_scatter x1, waiting for transfers between devices, body(): lax.psum_scatter(down_grad, 'dp', scatter_dimension=1, tiled=True)  141 us
    reduce_scatter x1, waiting for transfers between devices, body(): lax.psum_scatter(out_proj_grad, 'dp', scatter_dimension=1, tiled=True)  128 us
    unnamed x16, waiting for transfers between devices  101 us
    dot_general x24, matrix products, one_step(): jnp.einsum('qk,qd->kd', attn_probs.astype(jnp.bfloat16), ctx_block, prefe...  83 us
    all_gather x1, waiting for transfers between devices, body(): lax.all_gather(w_up, 'dp', axis=0, tiled=True)  60.2 us
    while x96, local copies, waits for them, and re-layouts  49 us
    all_gather x1, blocking collectives, body(): lax.all_gather(w_out, 'dp', axis=1, tiled=True)  48.6 us
  transfers between devices with their start and end apart: 15, of which 14 were waited for; matrix products, arithmetic and copies ran while one was open for 5% of the time, Pallas kernels for 0%

commit v1 on v0

--- a/solution.py
+++ b/solution.py
@@ -7,6 +7,12 @@
 LEN = 2048
 norm_eps = 1e-06
 masked_score = -1e30
+
+
+def open_state_now(buf, axis_name, ax_name):
+    for dev_j in (axis_name, ax_name):
+        buf = lax.psum(buf, axis_name=dev_j)
+    return buf
 
 
 def layer_norm(hidden, gain, shift):
@@ -212,8 +218,8 @@
         jnp.float32
     )
     spread_bias = own_slot[:, None] * bias_grad[None, :]
-    gain_sum, shift_sum, bias_sum = lax.psum(
-        (gain_grads, shift_grads, spread_bias), ("dp", "tensor")
+    gain_sum, shift_sum, bias_sum = open_state_now(
+        (gain_grads, shift_grads, spread_bias), "dp", "tensor"
     )
     bias_owned = jnp.sum(own_slot[:, None] * bias_sum, axis=0)
     return (

time: 1480 us -> 1480 us (level)
  waiting for transfers between devices: 727 us -> 687 us
  blocking collectives: 90.7 us -> 130 us
    unnamed x16, waiting for transfers between devices: 101 us -> 62 us
    psum x1 -> x2, blocking collectives: 42.1 us -> 81.4 us  [open_state_now(): buf = lax.psum(buf, axis_name=dev_j)]
where the time goes in v1:
time: 1480 us; the launch traced here: 1470 us
  waiting for transfers between devices  687 us (46%)
  matrix products  341 us (23%)
  local copies, waits for them, and re-layouts  154 us (10%)
  other arithmetic  136 us (9%)
  blocking collectives  130 us (9%)
  between operations  15.8 us (1%)
    reduce_scatter x1, waiting for transfers between devices, body(): lax.psum_scatter(up_grad, 'dp', scatter_dimension=0, tiled=True)  142 us
    reduce_scatter x1, waiting for transfers between devices, body(): lax.psum_scatter(down_grad, 'dp', scatter_dimension=1, tiled=True)  142 us
    reduce_scatter x1, waiting for transfers between devices, body(): lax.psum_scatter(out_proj_grad, 'dp', scatter_dimension=1, tiled=True)  129 us
    dot_general x24, matrix products, one_step(): jnp.einsum('qk,qd->kd', attn_probs.astype(jnp.bfloat16), ctx_block, prefe...  83 us
    psum x2, blocking collectives, open_state_now(): buf = lax.psum(buf, axis_name=dev_j)  81.4 us
    unnamed x16, waiting for transfers between devices  62 us
    all_gather x1, waiting for transfers between devices, body(): lax.all_gather(w_up, 'dp', axis=0, tiled=True)  60.2 us
    while x96, local copies, waits for them, and re-layouts  49 us
  transfers between devices with their start and end apart: 15, of which 14 were waited for; matrix products, arithmetic and copies ran while one was open for 5% of the time, Pallas kernels for 0%

profile of v1, /device:TPU:0, one launch (start us, length us, event | category | flops | bytes accessed | tf_op | source)
XLA Modules:
  0.0 1468.2 jit_solution(6563611922266266938)
XLA Ops:
  9.4 48.6 %all_gather.26 = bf16[384,768]{0,1:T(8,128)(2,1)} all-gather(bf16[384,48]{0,1:T(8,128)(2,1)} %param.23), channel_id=1, replica_groups=mesh['dp'=16,'tensor'=2] {'dp'}, dimensions={1}, use_global_device_ids=true | all-gather | bytes 626688 | tf_op jit(solution)/shard_map/all_gather | solution.py:113
  58.0 29.4 %all-gather.8.cloned.1.call-done = bf16[3,768,384]{2,1,0:T(8,128)(2,1)} async-done(((bf16[3,48,384]{2,1,0:T(8,128)(2,1)}), bf16[3,768,384]{2,1,0:T(8,128)(2,1)}) %all-gather.8.cloned.1.call-update) | async-done | bytes 1769488 | tf_op jit(solution)/shard_map/all_gather | solution.py:112
  87.4 9.9 fusion.61
  108.1 103.9 %while.51 = (s32[]{:T(128)}, bf16[6,2048,64]{1,2,0:T(8,128)(2,1)S(1)}, bf16[6,2048,64]{2,1,0:T(8,128)(2,1)}, bf16[6,2048,64]{2,1,0:T(8,128)(2,1)}, s32[6]{0:T(12...) while((s32[]{:T(128)}, bf16[6,2048,64]{1,2,0:T(8,128)(2,1)S(1)}, ...), condition=%wide.region_5.6_spmd, body=%wide.region_0.5_spmd.sunk | while | flops 277873664 | bytes 17058060 | solution.py:123
  111.1 13.8 while.54
  128.4 13.8 while.54
  145.7 13.8 while.54
  163.1 13.8 while.54
  180.4 13.8 while.54
  197.7 13.8 while.54
  212.1 6.0 fusion.62
  219.1 12.5 reduce-scatter.8.cloned.1.call-done
  237.9 60.2 %all-gather.14.cloned.1.call-done = bf16[768,1536]{1,0:T(8,128)(2,1)} async-done(((bf16[48,1536]{1,0:T(8,128)(2,1)}), bf16[768,1536]{1,0:T(8,128)(2,1)}) %all-gather.14.cloned.1.call-update) | async-done | bytes 2359312 | tf_op jit(solution)/shard_map/all_gather | solution.py:139
  298.1 13.0 all-gather.12.cloned.1.call-done
  311.1 34.9 %multiply_convert_fusion.1 = (bf16[2048,1536]{1,0:T(8,128)(2,1)}, f32[2048,1536]{1,0:T(8,128)}, f32[2048,1536]{1,0:T(8,128)}) fusion(f32[1536]{0:T(1024)S(1)} %convert_element_type.134, bf16[2048,768]{1,0:T(8,128)(2,1)} %all-gather.12.cloned.1.call-done, bf16[768,1536]{1,0:T(8,128)(2,1)} %all-gather.14.cloned.1.call-done), kind=kOutput, calls=%fused_computation.56 | convolution fusion | flops 5039456256 | bytes 36968448 | tf_op jit(solution)/shard_map/dot_general | solution.py:142
  346.0 31.7 %all-gather.16.cloned.1.call-done = bf16[1536,768]{0,1:T(8,128)(2,1)} async-done(((bf16[1536,48]{0,1:T(8,128)(2,1)}), bf16[1536,768]{0,1:T(8,128)(2,1)}) %all-gather.16.cloned.1.call-update) | async-done | bytes 2359312 | tf_op jit(solution)/shard_map/all_gather | solution.py:140
  377.6 9.6 fusion.63
  387.6 13.2 reduce-scatter.10.cloned.1.call-done
  413.3 13.4 all-gather.18.cloned.1.call-done
  426.6 17.6 %convert_reduce_fusion = (f32[1536]{0:T(1024)}, bf16[2048,1536]{1,0:T(8,128)(2,1)S(1)}) fusion(f32[2048,1536]{1,0:T(8,128)} %get-tuple-element.385, bf16[2048,768]{1,0:T(8,128)(2,1)} %all-gather.18.cloned.1.call-done, bf16[1536,768]{0,1:T(8,128)(2,1)} %all-gather.16.cloned.1.call-done, f32[2048,1536]{1,0:T(8,128)} %get-tuple-element.403, ...), kind=kOutput, calls=%fused_computation.54 | convolution fusion | flops 4885314048 | bytes 36974592 | tf_op jit(solution)/shard_map/rd,fd->rf/dot_general | solution.py:162
  446.9 6.9 fusion.64
  453.9 15.8 %reduce-scatter.12.cloned.1.call-done = f32[1024,768]{1,0:T(8,128)} async-done(((f32[2048,768]{1,0:T(8,128)}), f32[1024,768]{1,0:T(8,128)}) %reduce-scatter.12.cloned.1.call-update) | async-done | bytes 3145744 | tf_op jit(solution)/shard_map/reduce_scatter | solution.py:168
  469.6 4.3 multiply_reduce_fusion.1
  479.2 13.4 all-gather.20.cloned.1.call-done
  503.3 328.2 %while.53 = (s32[]{:T(128)}, bf16[6,2048,64]{1,2,0:T(8,128)(2,1)}, bf16[6,2048,64]{1,2,0:T(8,128)(2,1)}, bf16[6,2048,64]{1,2,0:T(8,128)(2,1)}, bf16[6,2048,64]{2...) while((s32[]{:T(128)}, bf16[6,2048,64]{1,2,0:T(8,128)(2,1)}, ...), condition=%wide.region_23.24_spmd, body=%wide.region_17.23_spmd.sunk | while | flops 692584960 | bytes 79334840 | solution.py:185
  508.2 47.7 %while.55 = (s32[]{:T(128)}, f32[2048,64]{0,1:T(8,128)S(1)}, f32[2048,64]{0,1:T(8,128)S(1)}, bf16[4,512,64]{1,2,0:T(8,128)(2,1)S(1)}, bf16[4,512,64]{2,1,0:T(8,1...) while((s32[]{:T(128)}, f32[2048,64]{0,1:T(8,128)S(1)}, ...), condition=%wide.region_22.22_spmd.clone, body=%wide.region_18.21_spmd.clone.sunk | while | flops 692584960 | bytes 73566400 | solution.py:97
  524.4 3.5 convolution_add_fusion.5
  536.4 3.5 convolution_add_fusion.5
  548.3 3.5 convolution_add_fusion.5
  562.9 47.7 %while.55 = (s32[]{:T(128)}, f32[2048,64]{0,1:T(8,128)S(1)}, f32[2048,64]{0,1:T(8,128)S(1)}, bf16[4,512,64]{1,2,0:T(8,128)(2,1)S(1)}, bf16[4,512,64]{2,1,0:T(8,1...) while((s32[]{:T(128)}, f32[2048,64]{0,1:T(8,128)S(1)}, ...), condition=%wide.region_22.22_spmd.clone, body=%wide.region_18.21_spmd.clone.sunk | while | flops 692584960 | bytes 73566400 | solution.py:97
  579.1 3.5 convolution_add_fusion.5
  591.1 3.5 convolution_add_fusion.5
  603.0 3.5 convolution_add_fusion.5
  617.6 47.7 %while.55 = (s32[]{:T(128)}, f32[2048,64]{0,1:T(8,128)S(1)}, f32[2048,64]{0,1:T(8,128)S(1)}, bf16[4,512,64]{1,2,0:T(8,128)(2,1)S(1)}, bf16[4,512,64]{2,1,0:T(8,1...) while((s32[]{:T(128)}, f32[2048,64]{0,1:T(8,128)S(1)}, ...), condition=%wide.region_22.22_spmd.clone, body=%wide.region_18.21_spmd.clone.sunk | while | flops 692584960 | bytes 73566400 | solution.py:97
  622.0 3.5 convolution_add_fusion.5
  633.9 3.5 convolution_add_fusion.5
  645.8 3.5 convolution_add_fusion.5
  657.7 3.5 convolution_add_fusion.5
  672.4 47.7 %while.55 = (s32[]{:T(128)}, f32[2048,64]{0,1:T(8,128)S(1)}, f32[2048,64]{0,1:T(8,128)S(1)}, bf16[4,512,64]{1,2,0:T(8,128)(2,1)S(1)}, bf16[4,512,64]{2,1,0:T(8,1...) while((s32[]{:T(128)}, f32[2048,64]{0,1:T(8,128)S(1)}, ...), condition=%wide.region_22.22_spmd.clone, body=%wide.region_18.21_spmd.clone.sunk | while | flops 692584960 | bytes 73566400 | solution.py:97
  676.7 3.5 convolution_add_fusion.5
  688.6 3.5 convolution_add_fusion.5
  700.5 3.5 convolution_add_fusion.5
  712.4 3.5 convolution_add_fusion.5
  727.0 47.7 %while.55 = (s32[]{:T(128)}, f32[2048,64]{0,1:T(8,128)S(1)}, f32[2048,64]{0,1:T(8,128)S(1)}, bf16[4,512,64]{1,2,0:T(8,128)(2,1)S(1)}, bf16[4,512,64]{2,1,0:T(8,1...) while((s32[]{:T(128)}, f32[2048,64]{0,1:T(8,128)S(1)}, ...), condition=%wide.region_22.22_spmd.clone, body=%wide.region_18.21_spmd.clone.sunk | while | flops 692584960 | bytes 73566400 | solution.py:97
  743.3 3.5 convolution_add_fusion.5
  755.2 3.5 convolution_add_fusion.5
  767.1 3.5 convolution_add_fusion.5
  781.7 47.7 %while.55 = (s32[]{:T(128)}, f32[2048,64]{0,1:T(8,128)S(1)}, f32[2048,64]{0,1:T(8,128)S(1)}, bf16[4,512,64]{1,2,0:T(8,128)(2,1)S(1)}, bf16[4,512,64]{2,1,0:T(8,1...) while((s32[]{:T(128)}, f32[2048,64]{0,1:T(8,128)S(1)}, ...), condition=%wide.region_22.22_spmd.clone, body=%wide.region_18.21_spmd.clone.sunk | while | flops 692584960 | bytes 73566400 | solution.py:97
  786.1 3.5 convolution_add_fusion.5
  809.9 3.5 convolution_add_fusion.5
  821.8 3.5 convolution_add_fusion.5
  837.9 8.2 multiply_bitcast_fusion
  846.0 6.3 copy.78
  852.6 7.1 fusion.50
  864.0 9.5 fusion.67
  875.4 9.6 fusion.66
  885.2 5.5 fusion.65
  892.1 77.4 %all-reduce.1 = (f32[2,768]{1,0:T(2,128)S(1)}, f32[4,768]{1,0:T(4,128)S(1)}, f32[2,1536]{1,0:T(2,128)S(1)}) all-reduce(f32[2,768]{1,0:T(2,128)S(1)} %pad_maximum_fusion.4, f32[4,768]{1,0:T(4,128)S(1)} %pad_maximum_fusion.3, f32[2,1536]{1,0:T(2,128)S(1)} %broadcast_multiply_fusion), channel_id=1, replica_groups=mesh['dp'=16,'tensor'=2] {'dp'}, use_global_device_ids=true, to_apply=%region_31.32 | all-reduce | flops 7680 | bytes 61440 | tf_op jit(solution)/shard_map/psum | solution.py:14
  969.5 4.0 all-reduce.2
  974.2 59.4 %all-reduce.5.cloned.1.call-done = f32[3,768,384]{2,0,1:T(4,128)} async-done(((f32[3,768,384]{2,0,1:T(4,128)}), f32[3,768,384]{2,0,1:T(4,128)}) %all-reduce.5.cloned.1.call-update) | async-done | bytes 3538960
  1035.3 10.9 reduce-scatter.14.cloned.1.call-done
  1049.7 141.5 %reduce-scatter.20.cloned.1.call-done = f32[1536,48]{0,1:T(8,128)} async-done(((f32[1536,768]{0,1:T(8,128)}), f32[1536,48]{0,1:T(8,128)}) %reduce-scatter.20.cloned.1.call-update) | async-done | bytes 294928 | tf_op jit(solution)/shard_map/reduce_scatter | solution.py:204
  1191.2 141.6 %reduce-scatter.18.cloned.1.call-done = f32[48,1536]{1,0:T(8,128)} async-done(((f32[768,1536]{1,0:T(8,128)}), f32[48,1536]{1,0:T(8,128)}) %reduce-scatter.18.cloned.1.call-update) | async-done | bytes 294928 | tf_op jit(solution)/shard_map/reduce_scatter | solution.py:203
  1332.8 128.7 %reduce-scatter.16.cloned.1.call-done = f32[384,48]{0,1:T(8,128)} async-done(((f32[384,768]{0,1:T(8,128)}), f32[384,48]{0,1:T(8,128)}) %reduce-scatter.16.cloned.1.call-update) | async-done | bytes 73744 | tf_op jit(solution)/shard_map/reduce_scatter | solution.py:202
  (619 shorter events, 430.4 us)
Async XLA Ops:
  7.2 50.8 %all-gather.10.cloned.1.call-start = ((), (), s32[]{:S(2)}) async-start(), calls=%async_computation.8 | async-start | bytes 4718592 | tf_op jit(solution)/shard_map/all_gather | solution.py:110
  7.9 79.5 %all-gather.8.cloned.1.call-start = ((), (), s32[]{:S(2)}) async-start(), calls=%async_computation.7 | async-start | bytes 1880064 | tf_op jit(solution)/shard_map/all_gather | solution.py:112
  8.7 222.9 %reduce-scatter.8.cloned.1.call-start = ((), (), s32[]{:S(2)}) async-start(), calls=%async_computation.9 | async-start | bytes 9437184 | tf_op jit(solution)/shard_map/reduce_scatter | solution.py:126
  212.1 6.0 copy-start.5
  212.1 6.0 copy-start.26
  218.1 80.0 %all-gather.14.cloned.1.call-start = ((), (), s32[]{:S(2)}) async-start(), calls=%async_computation.11 | async-start | bytes 2506752 | tf_op jit(solution)/shard_map/all_gather | solution.py:139
  218.7 92.4 %all-gather.12.cloned.1.call-start = ((), (), s32[]{:S(2)}) async-start(), calls=%async_computation.10 | async-start | bytes 4718592 | tf_op jit(solution)/shard_map/all_gather | solution.py:137
  235.5 2.4 copy-start.20
  237.2 140.4 %all-gather.16.cloned.1.call-start = ((), (), s32[]{:S(2)}) async-start(), calls=%async_computation.12 | async-start | bytes 2506752 | tf_op jit(solution)/shard_map/all_gather | solution.py:140
  237.8 163.0 %reduce-scatter.10.cloned.1.call-start = ((), (), s32[]{:S(2)}) async-start(), calls=%async_computation.13 | async-start | bytes 9437184 | tf_op jit(solution)/shard_map/reduce_scatter | solution.py:148
  387.3 39.3 %all-gather.18.cloned.1.call-start = ((), (), s32[]{:S(2)}) async-start(), calls=%async_computation.14 | async-start | bytes 4718592 | tf_op jit(solution)/shard_map/all_gather | solution.py:161
  413.2 56.4 %reduce-scatter.12.cloned.1.call-start = ((), (), s32[]{:S(2)}) async-start(), calls=%async_computation.15 | async-start | bytes 9437184 | tf_op jit(solution)/shard_map/reduce_scatter | solution.py:168
  426.6 20.2 %copy-start.24 = (bf16[768,1536]{1,0:T(8,128)(2,1)S(1)}, bf16[768,1536]{1,0:T(8,128)(2,1)}, u32[]{:S(2)}) copy-start(bf16[768,1536]{1,0:T(8,128)(2,1)} %all-gather.14.cloned.1.call-done) | copy-start | bytes 7077892
  444.2 2.7 copy-start.29
  453.8 20.1 %copy-start.11 = (f32[1024]{0:T(1024)S(1)}, f32[1024]{0:T(1024)}, u32[]{:S(2)}) copy-start(f32[1024]{0:T(1024)} %copy-done.10) | copy-start | bytes 12292
  453.8 38.8 %all-gather.20.cloned.1.call-start = ((), (), s32[]{:S(2)}) async-start(), calls=%async_computation.16 | async-start | bytes 4718592 | tf_op jit(solution)/shard_map/all_gather | solution.py:177
  475.4 3.7 copy-start.8
  477.0 15.6 %copy-start.7 = (bf16[384,768]{0,1:T(8,128)(2,1)S(1)}, bf16[384,768]{0,1:T(8,128)(2,1)}, u32[]{:S(2)}) copy-start(bf16[384,768]{0,1:T(8,128)(2,1)} %all_gather.26) | copy-start | bytes 1769476
  479.2 554.4 %all-reduce.5.cloned.1.call-start = ((), (), s32[]{:S(2)}) async-start(), calls=%async_computation.21 | async-start | bytes 9437184
  499.2 4.0 copy-start.27
  509.7 2.0 copy-start
  512.5 3.5 copy-start.1
  521.6 2.0 copy-start
  524.4 3.5 copy-start.1
  533.5 2.0 copy-start
  536.4 3.5 copy-start.1
  545.4 2.0 copy-start
  548.3 3.5 copy-start.1
  564.4 2.0 copy-start
  567.2 3.5 copy-start.1
  579.1 3.5 copy-start.1
  591.1 3.5 copy-start.1
  603.0 3.5 copy-start.1
  622.0 3.5 copy-start.1
  633.9 3.5 copy-start.1
  645.8 3.5 copy-start.1
  657.7 3.5 copy-start.1
  676.7 3.5 copy-start.1
  688.6 3.5 copy-start.1
  700.5 3.5 copy-start.1
  712.4 3.5 copy-start.1
  731.3 3.5 copy-start.1
  743.3 3.5 copy-start.1
  755.2 3.5 copy-start.1
  767.1 3.5 copy-start.1
  786.0 3.5 copy-start.1
  798.0 3.5 copy-start.1
  809.9 3.5 copy-start.1
  821.8 3.5 copy-start.1
  833.4 4.5 copy-start.28
  852.4 193.8 %reduce-scatter.14.cloned.1.call-start = ((), (), s32[]{:S(2)}) async-start(), calls=%async_computation.17 | async-start | bytes 4718592 | tf_op jit(solution)/shard_map/reduce_scatter | solution.py:208
  862.1 329.1 %reduce-scatter.20.cloned.1.call-start = ((), (), s32[]{:S(2)}) async-start(), calls=%async_computation.20 | async-start | bytes 5013504 | tf_op jit(solution)/shard_map/reduce_scatter | solution.py:204
  873.5 459.3 %reduce-scatter.18.cloned.1.call-start = ((), (), s32[]{:S(2)}) async-start(), calls=%async_computation.19 | async-start | bytes 5013504 | tf_op jit(solution)/shard_map/reduce_scatter | solution.py:203
  885.0 5.7 copy-start.25
  885.0 6.9 copy-start.16
  885.0 6.9 copy-start.15
  885.1 6.9 copy-start.14
  885.1 6.9 copy-start.18
  885.1 7.0 copy-start.17
  885.1 7.0 copy-start.13
  885.1 7.0 copy-start.12
  885.1 161.1 %copy-start.9 = (f32[1024]{0:T(1024)S(1)}, f32[1024]{0:T(1024)}, u32[]{:S(2)}) copy-start(f32[1024]{0:T(1024)} %copy-done.8) | copy-start | bytes 12292
  885.1 576.4 %reduce-scatter.16.cloned.1.call-start = ((), (), s32[]{:S(2)}) async-start(), calls=%async_computation.18 | async-start | bytes 1253376 | tf_op jit(solution)/shard_map/reduce_scatter | solution.py:202
  885.2 161.1 %copy-start.3 = (f32[1024,768]{1,0:T(8,128)S(1)}, f32[1024,768]{1,0:T(8,128)}, u32[]{:S(2)}) copy-start(f32[1024,768]{1,0:T(8,128)} %copy-done.2) | copy-start | bytes 9437188
  (27 other events, 49.5 us)
Sparse Core Ops, SparseCore 0:
  9.6 14.8 all-gather.9
  27.1 60.2 all-gather.7
  218.3 13.2 reduce-scatter.7
  234.6 63.4 all-gather.13
  300.1 10.9 all-gather.11
  314.1 63.4 all-gather.15
  387.4 13.3 reduce-scatter.9
  413.3 13.2 all-gather.17
  453.9 15.6 reduce-scatter.11
  479.3 13.2 all-gather.19
  852.5 181.0 all-reduce.4
  1036.2 9.9 reduce-scatter.13
  1052.8 138.3 reduce-scatter.19
  1196.8 135.9 reduce-scatter.17
  1338.7 122.7 reduce-scatter.15
